TPU v7x, 32 devices: a whole 2x2x4 slice. The times are simulated.
32 devices in a mesh: dp: 4 (over y, x), tensor: 8 (over z, core).
Axes of the slice: x: 2, y: 2, z: 4, core: 2. Of those that a mesh axis runs over, the one named last changes fastest.
Arguments:
- page_pool: bfloat16 [768, 1024, 256], P('dp', 'tensor'), may hold values from -5 to 5
- page_table: int32 [16, 64], P('dp'), may hold values from 0 to 191, as said below
- destination: int32 [16], replicated, may hold values from 0 to 15, as said below
- cache_len: int32 [16], replicated, may hold values from 2048 to 4096, as said below
- new_tokens: bfloat16 [16, 8192, 384], P('dp', 'tensor'), may hold values from -32 to 32
- residual_in: bfloat16 [8192, 2048], P(('dp', 'tensor')), may hold values from -48 to 48
- out_weight: bfloat16 [2048, 2048], P('tensor'), may hold values from -0.5 to 0.5
- norm_gain: float32 [2048], replicated, may hold values from 0.5 to 1.5
- routes: int32 [8192, 6], P(('dp', 'tensor')), may hold values from 0 to 63, all different within a row; in each aligned block of 256 rows (0 to 255, 256 to 511, ...) at most 32 rows name the same one
- route_gates: float32 [8192, 6], P(('dp', 'tensor')), may hold values from 0.1 to 1
- expert_gate: bfloat16 [64, 2048, 1408], P('tensor', None, 'dp'), may hold values from -0.125 to 0.125
- expert_up: bfloat16 [64, 2048, 1408], P('tensor', None, 'dp'), may hold values from -0.125 to 0.125
- expert_down: bfloat16 [64, 1408, 2048], P('tensor', 'dp'), may hold values from -0.15625 to 0.15625
Outputs:
- layer_out: float32 [8192, 2048], P(('dp', 'tensor'))
Inputs may be any that keep to these rules, and one draw needn't show every extreme that they name: `page_table`: each request names pages of its own dp index's pool of 192 pages; requests 2m and 2m + 1 of a dp index share the first half of their 64 pages, and no other page is named twice within a dp index. `destination`: A permutation of the serving slots; each dp index sends exactly one of its 4 requests to a slot of each other dp index and keeps the others in their own slots. `cache_len`: some request has exactly 4096 cached positions. `routes`: in the rows of one device (256 tokens) no expert is named more than 32 times.
All inputs are finite; a program needn't handle non-finite values.
Results may differ from a plain program's by a relative error of at most 0.004.
Values may be sent and summed in bfloat16 or wider, within the bound.
A program may use at most 256 MiB of HBM per device.

v0:
```python
import jax
import jax.numpy as jnp
from jax import lax
from jax.sharding import PartitionSpec as P

HEADS = 16
HD = 128
EXPERTS = 64
TOP = 6
PAGE = 64


def swapped(array, axis, stride):
    return lax.ppermute(array, axis, [(i, i ^ 1 << stride) for i in range(lax.axis_size(axis))])


def local_attention(queries, cached, fresh_rows, length, cache_offset, span_offset):
    head_size = queries.shape[1]
    span_len = queries.shape[0]
    page_count = cached.shape[0]
    page_rows = cached.shape[1]
    scale_factor = 1.0 / head_size**0.5
    cache_scores = jnp.einsum(
        "qd,pjd->qpj", queries, cached[:, :, :head_size], preferred_element_type=jnp.float32
    )
    cache_scores = cache_scores.reshape(span_len, page_count * page_rows) * scale_factor
    page_ids = jnp.arange(page_count, dtype=jnp.int32)[:, None]
    row_ids = jnp.arange(page_rows, dtype=jnp.int32)[None, :]
    positions = (page_ids * PAGE + cache_offset + row_ids).reshape(-1)
    cache_scores = jnp.where(positions[None, :] < length, cache_scores, -1e30)
    new_keys = fresh_rows[:, head_size : 2 * head_size]
    new_values = fresh_rows[:, 2 * head_size :]
    span_scores = jnp.dot(queries, new_keys.T, preferred_element_type=jnp.float32) * scale_factor
    key_pos = span_offset + jnp.arange(fresh_rows.shape[0], dtype=jnp.int32)
    query_pos = jnp.arange(span_len, dtype=jnp.int32)
    span_scores = jnp.where(key_pos[None, :] <= query_pos[:, None], span_scores, -1e30)
    maximum = jnp.maximum(jnp.max(cache_scores, axis=1), jnp.max(span_scores, axis=1))
    cache_weights = jnp.exp(cache_scores - maximum[:, None])
    span_weights = jnp.exp(span_scores - maximum[:, None])
    denominator = jnp.sum(cache_weights, axis=1) + jnp.sum(span_weights, axis=1)
    rounded = cache_weights.astype(jnp.bfloat16).reshape(span_len, page_count, page_rows)
    weighted = jnp.einsum(
        "qpj,pjd->qd", rounded, cached[:, :, head_size:], preferred_element_type=jnp.float32
    )
    weighted = weighted + jnp.dot(
        span_weights.astype(jnp.bfloat16), new_values, preferred_element_type=jnp.float32
    )
    return (weighted, maximum, denominator)


def run_experts(slot_rows, expert_gate, expert_up, expert_down):
    gate_part = jnp.einsum(
        "secd,edf->secf", slot_rows, expert_gate, preferred_element_type=jnp.float32
    )
    up_part = jnp.einsum("secd,edf->secf", slot_rows, expert_up, preferred_element_type=jnp.float32)
    active = (jax.nn.silu(gate_part) * up_part).astype(jnp.bfloat16)
    return jnp.einsum("secf,efd->secd", active, expert_down, preferred_element_type=jnp.float32)


def shards(
    page_pool,
    page_table,
    destination,
    cache_len,
    new_tokens,
    residual_in,
    out_weight,
    norm_gain,
    routes,
    route_gates,
    expert_gate,
    expert_up,
    expert_down,
):
    tensor_size = lax.axis_size("tensor")
    group_count = lax.axis_size("dp")
    split_ways = max(1, tensor_size // HEADS)
    heads_here = max(1, HEADS // tensor_size)
    side_index = lax.axis_index("tensor") % split_ways
    group_index = lax.axis_index("dp")
    requests_here = page_table.shape[0]
    first_home = group_index * requests_here
    home_dest = lax.dynamic_slice_in_dim(destination, first_home, requests_here)
    dest_group = home_dest // requests_here
    group_ids = jnp.arange(group_count, dtype=jnp.int32)
    request_ids = jnp.arange(requests_here, dtype=jnp.int32)
    leaving = dest_group[None, :] == group_ids[:, None]
    chosen = jnp.sum(jnp.where(leaving, request_ids[None, :], 0), axis=1)
    chosen = jnp.where(group_ids == group_index, 0, chosen)
    outgoing = page_pool[page_table[chosen]]
    arrived = lax.all_to_all(outgoing, "dp", split_axis=0, concat_axis=0, tiled=True)
    inverse = (
        jnp.zeros_like(destination)
        .at[destination]
        .set(jnp.arange(destination.shape[0], dtype=jnp.int32))
    )
    served = lax.dynamic_slice_in_dim(inverse, first_home, requests_here)
    source = served // requests_here
    resident = source == group_index
    local_pages = page_pool[page_table[jnp.where(resident, served - first_home, 0)]]
    dense_cache = jnp.where(resident[:, None, None, None], local_pages, arrived[source])
    lengths = cache_len[served]
    fresh_per = new_tokens.shape[1] // heads_here
    span_len = fresh_per * split_ways
    rows_per_head = dense_cache.shape[2] // heads_here
    if split_ways == 2:
        own_queries = new_tokens[:, :, :HD]
        other_queries = swapped(own_queries, "tensor", 0)
        lower_half = jnp.where(side_index == 0, own_queries, other_queries)
        upper_half = jnp.where(side_index == 0, other_queries, own_queries)
        queries = jnp.concatenate([lower_half, upper_half], axis=1)[:, None]
    else:
        queries = new_tokens[:, :, :HD].reshape(requests_here, heads_here, span_len, HD)
    head_results = []
    for head_index in range(heads_here):
        head_cache = dense_cache[
            :, :, head_index * rows_per_head : (head_index + 1) * rows_per_head
        ]
        head_fresh = new_tokens[:, head_index * fresh_per : (head_index + 1) * fresh_per]

        def one_request(operands):
            return local_attention(
                operands[0],
                operands[1],
                operands[2],
                operands[3],
                side_index * rows_per_head,
                side_index * fresh_per,
            )

        head_results.append(
            lax.map(one_request, (queries[:, head_index], head_cache, head_fresh, lengths))
        )
    if split_ways == 2:
        weighted, maximum, denominator = head_results[0]
        half_dim = HD // 2
        given_part = lax.dynamic_slice_in_dim(weighted, (1 - side_index) * half_dim, half_dim, 2)
        kept_part = lax.dynamic_slice_in_dim(weighted, side_index * half_dim, half_dim, 2)
        received_part, other_max, other_den = swapped(
            (given_part, maximum, denominator), "tensor", 0
        )
        joint_max = jnp.maximum(maximum, other_max)
        own_scale = jnp.exp(maximum - joint_max)
        theirs = jnp.exp(other_max - joint_max)
        combined = kept_part * own_scale[..., None] + received_part * theirs[..., None]
        attended = combined / (denominator * own_scale + other_den * theirs)[..., None]
        head_out = attended.astype(jnp.bfloat16).reshape(requests_here * span_len, half_dim)
    else:
        outputs = []
        for result in head_results:
            outputs.append((result[0] / result[2][..., None]).astype(jnp.bfloat16))
        head_out = jnp.stack(outputs, axis=2).reshape(requests_here * span_len, heads_here * HD)
    tok_rows = residual_in.shape[0]
    projected = lax.psum_scatter(
        jnp.dot(head_out, out_weight, preferred_element_type=jnp.float32),
        "tensor",
        scatter_dimension=0,
        tiled=True,
    )
    hidden = residual_in.astype(jnp.float32) + projected
    normed = (
        hidden * lax.rsqrt(jnp.mean(hidden * hidden, axis=1, keepdims=True) + 1e-06) * norm_gain
    ).astype(jnp.bfloat16)
    capacity = max(2, tok_rows * TOP * 4 // (3 * EXPERTS))
    flat_routes = routes.reshape(-1)
    pair_count = flat_routes.shape[0]
    expert_ids = jnp.arange(EXPERTS, dtype=jnp.int32)
    one_hot = (flat_routes[:, None] == expert_ids[None, :]).astype(jnp.int32)
    earlier = jnp.cumsum(one_hot, axis=0) - one_hot
    rank_in_expert = jnp.sum(earlier * one_hot, axis=1)
    slot_of_pair = flat_routes * capacity + rank_in_expert
    slot_ids = jnp.arange(EXPERTS * capacity, dtype=jnp.int32)
    matches = slot_of_pair[None, :] == slot_ids[:, None]
    source_pair = jnp.sum(
        jnp.where(matches, jnp.arange(pair_count, dtype=jnp.int32)[None, :], 0), axis=1
    )
    filled = jnp.any(matches, axis=1)
    outgoing_rows = jnp.where(
        filled[:, None], normed[source_pair // TOP], jnp.zeros((), jnp.bfloat16)
    )
    experts_here = expert_gate.shape[0]
    width = normed.shape[1]
    outgoing_rows = outgoing_rows.reshape(tensor_size, experts_here, capacity, width)
    fanned = jnp.broadcast_to(outgoing_rows[None], (group_count,) + outgoing_rows.shape)
    fanned = fanned.reshape((group_count * tensor_size,) + outgoing_rows.shape[1:])
    partial_value = run_experts(
        lax.all_to_all(fanned, ("dp", "tensor"), split_axis=0, concat_axis=0, tiled=True),
        expert_gate,
        expert_up,
        expert_down,
    ).astype(jnp.bfloat16)
    returned = lax.all_to_all(
        partial_value, ("dp", "tensor"), split_axis=0, concat_axis=0, tiled=True
    )
    slot_out = jnp.sum(
        returned.reshape(group_count, EXPERTS * capacity, width).astype(jnp.float32), axis=0
    )
    picked = slot_out[slot_of_pair].reshape(tok_rows, TOP, width)
    routed = jnp.sum(picked * route_gates[:, :, None], axis=1)
    return hidden + routed


def solution(mesh):
    return jax.shard_map(
        shards,
        mesh=mesh,
        in_specs=(
            P("dp", "tensor", None),
            P("dp", None),
            P(),
            P(),
            P("dp", "tensor", None),
            P(("dp", "tensor"), None),
            P("tensor", None),
            P(),
            P(("dp", "tensor"), None),
            P(("dp", "tensor"), None),
            P("tensor", None, "dp"),
            P("tensor", None, "dp"),
            P("tensor", "dp", None),
        ),
        out_specs=P(("dp", "tensor"), None),
        check_vma=False,
    )
```

profile of v0, /device:TPU:0, one launch (start us, length us, event | category | flops | bytes accessed | tf_op | source)
XLA Modules:
  0.0 2355.4 jit_solution(16344600266283102921)
XLA Ops:
  10.2 14.1 gather_fusion.4
  32.2 14.3 gather_fusion.2
  52.0 163.4 %all-to-all-done = bf16[4,64,128,256]{3,2,1,0:T(8,128)(2,1)} async-done(((bf16[4,64,128,256]{3,2,1,0:T(8,128)(2,1)}), bf16[4,64,128,256]{3,2,1,0:T(8,128)(2,1)}, u32[]{:S(2)}, u32[]{:S(2)}) %all-to-all-start) | async-done | bytes 16777248 | tf_op jit(solution)/shard_map/all_to_all | solution.py:91
  215.4 11.9 fusion.81
  232.7 17.5 while.34
  255.5 17.1 while.35
  272.7 14.2 maximum_select_fusion
  294.7 103.3 %while.32 = (s32[]{:T(128)}, f32[4,512,128]{2,1,0:T(8,128)}, f32[4,512]{1,0:T(4,128)}, s32[4]{0:T(128)S(1)}, bf16[4,512,128]{2,1,0:T(8,128)(2,1)}, /*index=5*/bf...) while((s32[]{:T(128)}, f32[4,512,128]{2,1,0:T(8,128)}, ...), condition=%wide.region_7.8_spmd, body=%wide.region_2.7_spmd.sunk | while | flops 1226906624 | bytes 55627952 | solution.py:132
  399.7 104.7 %while.33 = (s32[]{:T(128)}, f32[4,512,128]{2,1,0:T(8,128)}, f32[4,512]{1,0:T(4,128)}, s32[4]{0:T(128)S(1)}, bf16[4,512,128]{2,1,0:T(8,128)(2,1)}, /*index=5*/bf...) while((s32[]{:T(128)}, f32[4,512,128]{2,1,0:T(8,128)}, ...), condition=%wide.region_13.14_spmd, body=%wide.region_8.13_spmd.sunk | while | flops 1226906624 | bytes 55627952 | solution.py:132
  508.7 8.1 fusion.61
  518.0 18.4 reduce-window.6
  540.4 145.1 %reduce-scatter.2.cloned.1.call-done = f32[256,2048]{1,0:T(8,128)} async-done(((f32[2048,2048]{1,0:T(8,128)}), f32[256,2048]{1,0:T(8,128)}) %reduce-scatter.2.cloned.1.call-update) | async-done | bytes 2097168 | tf_op jit(solution)/shard_map/reduce_scatter | solution.py:154
  689.4 11.0 gather_fusion.5
  700.4 7.3 broadcast_select_fusion
  707.7 13.5 broadcast_in_dim.181
  721.1 729.7 %all_to_all.15 = bf16[32,8,32,2048]{3,2,1,0:T(8,128)(2,1)} all-to-all(bf16[32,8,32,2048]{3,2,1,0:T(8,128)(2,1)} %bitcast.212), channel_id=1, replica_groups=mesh['dp'=4,'tensor'=8] {'dp','tensor'}, dimensions={0} | all-to-all | bytes 67108864 | tf_op jit(solution)/shard_map/all_to_all | solution.py:187
  1450.8 27.6 %fusion.40 = f32[8,32,32,352]{3,2,1,0:T(8,128)} fusion(bf16[32,8,32,2048]{3,2,1,0:T(8,128)(2,1)} %all_to_all.15, bf16[8,2048,352]{1,2,0:T(8,128)(2,1)} %param.28), kind=kOutput, calls=%fused_computation.74 | convolution fusion | flops 11811160064 | bytes 56623104 | tf_op jit(solution)/shard_map/secd,edf->secf/dot_general | solution.py:55
  1478.4 49.0 %convert_bitcast_fusion = bf16[32,8,32,2048]{3,2,0,1:T(8,128)(2,1)} fusion(bf16[8,352,2048]{2,1,0:T(8,128)(2,1)} %param.29, f32[8,32,32,352]{3,2,1,0:T(8,128)} %fusion.40, bf16[8,2048,352]{1,2,0:T(8,128)(2,1)} %param.27, bf16[32,8,32,2048]{3,2,1,0:T(8,128)(2,1)} %all_to_all.15), kind=kOutput, calls=%fused_computation.73 | convolution fusion | flops 23656398848 | bytes 101711872 | tf_op jit(solution)/shard_map/secf,efd->secd/dot_general | solution.py:57
  1527.4 22.9 copy.58
  1555.5 723.7 %all-to-all-done.2 = bf16[32,8,32,2048]{3,2,1,0:T(8,128)(2,1)} async-done(((bf16[32,8,32,2048]{3,2,1,0:T(8,128)(2,1)}), bf16[32,8,32,2048]{3,2,1,0:T(8,128)(2,1)}, u32[]{:S(2)}, u32[]{:S(2)}) %all-to-all-start.2) | async-done | bytes 33554464 | tf_op jit(solution)/shard_map/all_to_all | solution.py:192
  2279.1 24.6 %convert_reduce_fusion = f32[2048,2048]{1,0:T(8,128)} fusion(bf16[4,2048,2048]{2,1,0:T(8,128)(2,1)} %bitcast.51), kind=kLoop, calls=%fused_computation.72 | loop fusion | flops 29360128 | bytes 50331648 | tf_op jit(solution)/shard_map/reduce_sum | solution.py:195
  2303.7 18.3 gather_fusion.6
  2322.0 15.0 reshape.353
  2337.0 9.5 multiply_reduce_fusion
  (276 shorter events, 299.6 us)
Async XLA Ops:
  6.5 502.2 %copy-start = (bf16[256,2048]{1,0:T(8,128)(2,1)S(1)}, bf16[256,2048]{1,0:T(8,128)(2,1)}, u32[]{:S(2)}) copy-start(bf16[256,2048]{1,0:T(8,128)(2,1)} %param.23) | copy-start | bytes 3145732
  24.4 7.2 copy-start.10
  24.4 191.1 %all-to-all-start = ((bf16[4,64,128,256]{3,2,1,0:T(8,128)(2,1)}), bf16[4,64,128,256]{3,2,1,0:T(8,128)(2,1)}, u32[]{:S(2)}, u32[]{:S(2)}) async-start(bf16[4,64,128,256]{3,2,1,0:T(8,128)(2,1)} %bitcast.218), calls=%async_computation | async-start | bytes 33554432 | tf_op jit(solution)/shard_map/all_to_all | solution.py:91
  31.5 654.0 %reduce-scatter.2.cloned.1.call-start = ((), (), s32[]{:S(2)}) async-start(), calls=%async_computation.4 | async-start | bytes 18874368 | tf_op jit(solution)/shard_map/reduce_scatter | solution.py:154
  32.2 14.3 copy-start.2
  32.2 14.9 slice-start
  304.1 3.9 copy-start.3
  329.9 3.9 copy-start.3
  355.7 3.9 copy-start.3
  381.5 3.9 copy-start.3
  409.5 3.9 copy-start.5
  435.6 3.9 copy-start.5
  461.7 3.9 copy-start.5
  487.8 3.9 copy-start.5
  516.8 168.7 %copy-start.8 = (bf16[256,2048]{1,0:T(8,128)(2,1)S(1)}, bf16[256,2048]{1,0:T(8,128)(2,1)}, u32[]{:S(2)}) copy-start(bf16[256,2048]{1,0:T(8,128)(2,1)} %param.22) | copy-start | bytes 3145732
  517.5 170.0 %copy-start.15 = (f32[2048]{0:T(1024)S(1)}, f32[2048]{0:T(1024)}, u32[]{:S(2)}) copy-start(f32[2048]{0:T(1024)} %param.24) | copy-start | bytes 24580
  537.3 163.1 %copy-start.11 = (s32[1536]{0:T(1024)}, s32[1536]{0:T(1024)S(1)}, u32[]{:S(2)}) copy-start(s32[1536]{0:T(1024)S(1)} %fusion.70) | copy-start | bytes 18436
  1550.3 4.6 copy-start.14
  1550.3 5.0 copy-start.16
  1550.3 5.1 copy-start.12
  1550.3 728.8 %all-to-all-start.2 = ((bf16[32,8,32,2048]{3,2,1,0:T(8,128)(2,1)}), bf16[32,8,32,2048]{3,2,1,0:T(8,128)(2,1)}, u32[]{:S(2)}, u32[]{:S(2)}) async-start(bf16[32,8,32,2048]{3,2,1,0:T(8,128)(2,1)} %copy.58), calls=%async_computation.3 | async-start | bytes 67108864 | tf_op jit(solution)/shard_map/all_to_all | solution.py:192
  2337.0 9.5 copy-start.7
  2337.0 9.6 copy-start.9
  2337.0 11.3 copy-start.1
  (9 other events, 29.2 us)
Sparse Core Ops, SparseCore 0:
  516.9 168.5 reduce-scatter.1
where the time goes:
time: 2360 us
  waiting for transfers between devices  1030 us (44%)
  blocking collectives  730 us (31%)
  local copies, waits for them, and re-layouts  287 us (12%)
  matrix products  154 us (7%)
  other arithmetic  126 us (5%)
    all_to_all x1, blocking collectives, shards(): lax.all_to_all(fanned, ('dp', 'tensor'), split_axis=0, concat_axis=0, til...  730 us
    all_to_all x1, waiting for transfers between devices, shards(): lax.all_to_all(partial_value, ('dp', 'tensor'), split_axis=0, concat_axis...  724 us
    all_to_all x1, waiting for transfers between devices, shards(): lax.all_to_all(outgoing, 'dp', split_axis=0, concat_axis=0, tiled=True)  163 us
    reduce_scatter x1, waiting for transfers between devices, shards(): lax.psum_scatter(jnp.dot(head_out, out_weight, preferred_element_type=jnp...  145 us
    convert_element_type x8, local copies, waits for them, and re-layouts, local_attention(): cache_weights.astype(jnp.bfloat16).reshape(span_len, page_count, page_rows)  51.7 us
    dot_general x1, matrix products, run_experts(): jnp.einsum('secf,efd->secd', active, expert_down, preferred_element_type=...  49 us
  transfers between devices with their start and end apart: 3, of which 3 were waited for; matrix products, arithmetic and copies ran while one was open for 2% of the time, Pallas kernels for 0%

commit v1 on v0

--- a/solution.py
+++ b/solution.py
@@ -1,6 +1,8 @@
 import jax
 import jax.numpy as jnp
 from jax import lax
+from jax.experimental import pallas as pl
+from jax.experimental.pallas import tpu as pltpu
 from jax.sharding import PartitionSpec as P
 
 HEADS = 16
@@ -200,9 +202,288 @@
     return hidden + routed
 
 
+def exchanged(blocks, axis):
+    return lax.all_to_all(blocks, axis, split_axis=0, concat_axis=0, tiled=True)
+
+
+def attention_kernel(
+    table_ref, length_ref, pool_ref, fresh_ref, out_ref, pages, top, total, arrival, *, heads, step
+):
+    turn = pl.program_id(0)
+    page_count = pages.shape[1]
+    span_len = fresh_ref.shape[1] // heads
+    scale_factor = 1.4426950408889634 / HD**0.5
+
+    def fetch(request, slot):
+        def one_page(page, carry):
+            pltpu.make_async_copy(
+                pool_ref.at[table_ref[request, page]], pages.at[slot, page], arrival.at[slot]
+            ).start()
+            return carry
+
+        lax.fori_loop(0, page_count, one_page, 0)
+
+    @pl.when(turn == 0)
+    def _():
+        fetch(0, 0)
+
+    @pl.when(turn + 1 < pl.num_programs(0))
+    def _():
+        fetch(turn + 1, (turn + 1) % 2)
+
+    slot = turn % 2
+    length = length_ref[turn]
+
+    def query_of(head):
+        return fresh_ref[0, head * span_len : (head + 1) * span_len, :HD]
+
+    def scores_of(head, keys):
+        return (
+            lax.dot_general(
+                query_of(head), keys, (((1,), (1,)), ((), ())), preferred_element_type=jnp.float32
+            )
+            * scale_factor
+        )
+
+    def weighted_of(weights, values):
+        widened = jnp.concatenate([values, jnp.ones_like(values)], axis=1)
+        return jnp.dot(
+            weights.astype(jnp.bfloat16), widened, preferred_element_type=jnp.float32
+        )
+
+    for head in range(heads):
+        rows = slice(head * span_len, (head + 1) * span_len)
+        scores = scores_of(head, fresh_ref[0, rows, HD : 2 * HD])
+        query_pos = lax.broadcasted_iota(jnp.int32, scores.shape, 0)
+        key_pos = lax.broadcasted_iota(jnp.int32, scores.shape, 1)
+        scores = jnp.where(key_pos <= query_pos, scores, -1e30)
+        largest = jnp.max(scores, axis=1, keepdims=True)
+        top[head] = jnp.broadcast_to(largest, top.shape[1:])
+        total[head] = weighted_of(jnp.exp2(scores - largest), fresh_ref[0, rows, 2 * HD :])
+
+    pltpu.make_async_copy(
+        pool_ref.at[pl.ds(0, page_count)], pages.at[slot], arrival.at[slot]
+    ).wait()
+
+    def chunk(index, masked):
+        for head in range(heads):
+            block = pages[slot, pl.ds(index * step, step), head * PAGE : (head + 1) * PAGE, :]
+            block = block.reshape(step * PAGE, 2 * HD)
+            scores = scores_of(head, block[:, :HD])
+            if masked:
+                key_pos = index * (step * PAGE) + lax.broadcasted_iota(jnp.int32, scores.shape, 1)
+                scores = jnp.where(key_pos < length, scores, -1e30)
+            before = top[head][:, :1]
+            largest = jnp.maximum(before, jnp.max(scores, axis=1, keepdims=True))
+            weighted = weighted_of(jnp.exp2(scores - largest), block[:, HD:])
+            total[head] = total[head] * jnp.exp2(before - largest) + weighted
+            top[head] = jnp.broadcast_to(largest, top.shape[1:])
+
+    whole = length // (step * PAGE)
+
+    def one_chunk(index, carry):
+        chunk(index, False)
+        return carry
+
+    lax.fori_loop(0, whole, one_chunk, 0)
+
+    @pl.when(whole * (step * PAGE) < length)
+    def _():
+        chunk(whole, True)
+
+    for head in range(heads):
+        joined = total[head]
+        out_ref[0, :, head * HD : (head + 1) * HD] = (joined[:, :HD] / joined[:, HD:]).astype(
+            out_ref.dtype
+        )
+
+
+def paged_attention(page_pool, table, lengths, fresh, heads):
+    requests, page_count = table.shape
+    span_len = fresh.shape[1] // heads
+    step = max(size for size in (1, 2, 4, 8, 16) if page_count % size == 0)
+    return pl.pallas_call(
+        lambda *refs: attention_kernel(*refs, heads=heads, step=step),
+        out_shape=jax.ShapeDtypeStruct((requests, span_len, heads * HD), jnp.bfloat16),
+        grid_spec=pltpu.PrefetchScalarGridSpec(
+            num_scalar_prefetch=2,
+            grid=(requests,),
+            in_specs=[
+                pl.BlockSpec(memory_space=pl.ANY),
+                pl.BlockSpec((1,) + fresh.shape[1:], lambda i, *_: (i, 0, 0)),
+            ],
+            out_specs=pl.BlockSpec((1, span_len, heads * HD), lambda i, *_: (i, 0, 0)),
+            scratch_shapes=[
+                pltpu.VMEM((2, page_count) + page_pool.shape[1:], jnp.bfloat16),
+                pltpu.VMEM((heads, span_len, HD), jnp.float32),
+                pltpu.VMEM((heads, span_len, 2 * HD), jnp.float32),
+                pltpu.SemaphoreType.DMA((2,)),
+            ],
+        ),
+        compiler_params=pltpu.CompilerParams(vmem_limit_bytes=48 * 2**20),
+    )(table, lengths, page_pool, fresh)
+
+
+def expert_kernel(
+    rank_ref, weight_ref, rows_ref, gate_ref, up_ref, down_ref, out_ref, held, *, capacity
+):
+    expert = pl.program_id(1)
+    sources, experts, tokens = rank_ref.shape
+    width = rows_ref.shape[1]
+
+    def placement(source):
+        ranks = rank_ref[source]
+        places = lax.broadcasted_iota(jnp.int32, (experts, capacity, tokens), 1).astype(jnp.float32)
+        hits = jnp.where(ranks[:, None, :] == places, 1.0, 0.0)
+        return hits.reshape(experts * capacity, tokens).astype(jnp.bfloat16)
+
+    def slots_of(source):
+        return pl.ds(pl.multiple_of(source * capacity, capacity), capacity)
+
+    def rows_of(source):
+        return pl.ds(pl.multiple_of(source * tokens, tokens), tokens)
+
+    @pl.when(expert == 0)
+    def _():
+        def gather(source, carry):
+            picked = jnp.dot(
+                placement(source), rows_ref[rows_of(source), :], preferred_element_type=jnp.float32
+            ).astype(jnp.bfloat16)
+            held[:, slots_of(source), :] = picked.reshape(experts, capacity, width)
+            return carry
+
+        lax.fori_loop(0, sources, gather, 0)
+
+    chosen = held[expert]
+    gate_part = jnp.dot(chosen, gate_ref[0], preferred_element_type=jnp.float32)
+    up_part = jnp.dot(chosen, up_ref[0], preferred_element_type=jnp.float32)
+    active = (gate_part / (1.0 + jnp.exp(-gate_part)) * up_part).astype(jnp.bfloat16)
+    ranks = rank_ref[:, pl.ds(expert, 1), :]
+    weights = weight_ref[:, pl.ds(expert, 1), :]
+    places = lax.broadcasted_iota(jnp.int32, (sources, capacity, tokens), 1).astype(jnp.float32)
+    slot_weight = jnp.sum(jnp.where(ranks == places, weights, 0.0), axis=2, keepdims=True)
+    partial_value = jnp.dot(active, down_ref[0], preferred_element_type=jnp.float32)
+    scaled = partial_value * slot_weight.reshape(sources * capacity, 1)
+    held[expert] = scaled.astype(jnp.bfloat16)
+
+    @pl.when(expert == experts - 1)
+    def _():
+        def combine(source, carry):
+            parts = held[:, slots_of(source), :].reshape(experts * capacity, width)
+            out_ref[rows_of(source), :] = lax.dot_general(
+                placement(source),
+                parts,
+                (((0,), (0,)), ((), ())),
+                preferred_element_type=jnp.float32,
+            ).astype(out_ref.dtype)
+            return carry
+
+        lax.fori_loop(0, sources, combine, 0)
+
+
+def routed_experts(ranks, weights, rows, expert_gate, expert_up, expert_down, capacity):
+    sources, experts, tokens = ranks.shape
+    width = rows.shape[1]
+    hidden_units = expert_gate.shape[2]
+    together = max(size for size in (1, 2, 4, 8) if sources % size == 0)
+    return pl.pallas_call(
+        lambda *refs: expert_kernel(*refs, capacity=capacity),
+        out_shape=jax.ShapeDtypeStruct(rows.shape, jnp.bfloat16),
+        grid=(sources // together, experts),
+        in_specs=[
+            pl.BlockSpec((together, experts, tokens), lambda i, j: (i, 0, 0)),
+            pl.BlockSpec((together, experts, tokens), lambda i, j: (i, 0, 0)),
+            pl.BlockSpec((together * tokens, width), lambda i, j: (i, 0)),
+            pl.BlockSpec((1, width, hidden_units), lambda i, j: (j, 0, 0)),
+            pl.BlockSpec((1, width, hidden_units), lambda i, j: (j, 0, 0)),
+            pl.BlockSpec((1, hidden_units, width), lambda i, j: (j, 0, 0)),
+        ],
+        out_specs=pl.BlockSpec((together * tokens, width), lambda i, j: (i, 0)),
+        scratch_shapes=[pltpu.VMEM((experts, together * capacity, width), jnp.bfloat16)],
+        compiler_params=pltpu.CompilerParams(vmem_limit_bytes=60 * 2**20),
+    )(ranks, weights, rows, expert_gate, expert_up, expert_down)
+
+
+def home_shards(
+    page_pool,
+    page_table,
+    destination,
+    cache_len,
+    new_tokens,
+    residual_in,
+    out_weight,
+    norm_gain,
+    routes,
+    route_gates,
+    expert_gate,
+    expert_up,
+    expert_down,
+):
+    both = ("dp", "tensor")
+    tensor_index = lax.axis_index("tensor")
+    group_index = lax.axis_index("dp")
+    heads_here = HEADS // lax.axis_size("tensor")
+    requests_here = page_table.shape[0]
+    first_home = group_index * requests_here
+    group_ids = jnp.arange(requests_here, dtype=jnp.int32)
+
+    home_dest = lax.dynamic_slice_in_dim(destination, first_home, requests_here)
+    to_group = (home_dest // requests_here)[None, :] == group_ids[:, None]
+    request_of = jnp.sum(jnp.where(to_group, group_ids[None, :], 0), axis=1)
+    all_ids = jnp.arange(destination.shape[0], dtype=jnp.int32)
+    slot_ids = first_home + group_ids
+    served = jnp.sum(
+        jnp.where(destination[None, :] == slot_ids[:, None], all_ids[None, :], 0), axis=1
+    )
+    source = served // requests_here
+    slot_of = jnp.sum(
+        jnp.where(source[None, :] == group_ids[:, None], group_ids[None, :], 0), axis=1
+    )
+
+    fresh = exchanged(new_tokens[slot_of], "dp")
+    lengths = cache_len[first_home + request_of]
+    attended = paged_attention(page_pool, page_table[request_of], lengths, fresh, heads_here)
+    span_len, head_width = attended.shape[1:]
+    by_slot = exchanged(attended, "dp")[source]
+    by_slot = by_slot.reshape(requests_here * span_len, head_width)
+
+    tok_rows, width = residual_in.shape
+    whole_weight = lax.all_gather(out_weight, "tensor", axis=0, tiled=True)
+    head_out = lax.all_to_all(by_slot, "tensor", split_axis=0, concat_axis=1, tiled=True)
+    projected = jnp.dot(head_out, whole_weight, preferred_element_type=jnp.float32)
+    hidden = residual_in.astype(jnp.float32) + projected
+    normed = (
+        hidden * lax.rsqrt(jnp.mean(hidden * hidden, axis=1, keepdims=True) + 1e-06) * norm_gain
+    ).astype(jnp.bfloat16)
+
+    capacity = max(2, tok_rows * TOP * 4 // (3 * EXPERTS))
+    experts_here = expert_gate.shape[0]
+    all_routes = lax.all_gather(routes.T, both, axis=0, tiled=False)
+    all_gates = lax.all_gather(route_gates.T, both, axis=0, tiled=False)
+    own_experts = tensor_index * experts_here + jnp.arange(experts_here, dtype=jnp.int32)
+    named = all_routes[:, None] == own_experts[None, :, None, None]
+    weights = jnp.sum(jnp.where(named, all_gates[:, None], 0.0), axis=2)
+    hit = jnp.any(named, axis=2)
+    token_ids = jnp.arange(tok_rows, dtype=jnp.int32)
+    before = (token_ids[:, None] < token_ids[None, :]).astype(jnp.bfloat16)
+    ranks = jnp.einsum(
+        "set,tu->seu", hit.astype(jnp.bfloat16), before, preferred_element_type=jnp.float32
+    )
+    ranks = jnp.where(hit, ranks, -1.0)
+
+    rows = lax.all_gather(normed, both, axis=0, tiled=True)
+    partial_value = routed_experts(
+        ranks, weights, rows, expert_gate, expert_up, expert_down, capacity
+    )
+    routed = lax.psum_scatter(partial_value, both, scatter_dimension=0, tiled=True)
+    return hidden + routed.astype(jnp.float32)
+
+
 def solution(mesh):
+    sizes = dict(mesh.shape)
+    own_heads = HEADS % sizes["tensor"] == 0
     return jax.shard_map(
-        shards,
+        home_shards if own_heads else shards,
         mesh=mesh,
         in_specs=(
             P("dp", "tensor", None),

time: 2360 us -> 824 us (0.35)
  blocking collectives: 730 us -> 113 us
  waiting for transfers between devices: 1030 us -> 487 us
  local copies, waits for them, and re-layouts: 287 us -> 37.9 us
  matrix products: 154 us -> 6.97 us
  Pallas kernels: 0 us -> 143 us
  other arithmetic: 126 us -> 7.7 us
    all_to_all x2, waiting for transfers between devices: 887 us -> 47.2 us  [exchanged(): return lax.all_to_all(blocks, axis, split_axis=0, concat_axis=0, tiled=True)]
    all_to_all x1, blocking collectives: 730 us -> 31.9 us  [home_shards(): lax.all_to_all(by_slot, 'tensor', split_axis=0, concat_axis=1, tiled=True)]
    reduce_scatter x1, waiting for transfers between devices: 145 us -> 360 us  [home_shards(): lax.psum_scatter(partial_value, both, scatter_dimension=0, tiled=True)]
    dot_general x35 -> x2, matrix products: 154 us -> 6.97 us  [the longest x1 6.07 us: home_shards(): jnp.dot(head_out, whole_weight, preferred_element_type=jnp.float32)]
    pallas_call x0 -> x2, Pallas kernels: none -> 143 us  [the longest x1 104 us: routed_experts(): pl.pallas_call(lambda *refs: expert_kernel(*refs, capacity=capacity), out...]
    gather x24 -> x4, local copies, waits for them, and re-layouts: 107 us -> 4.53 us  [the longest x1 2.72 us: home_shards(): fresh = exchanged(new_tokens[slot_of], 'dp')]
    all_gather x0 -> x2, blocking collectives: none -> 81.6 us  [the longest x1 41.2 us: home_shards(): all_routes = lax.all_gather(routes.T, both, axis=0, tiled=False)]
    all_gather x0 -> x2, waiting for transfers between devices: none -> 79.4 us  [the longest x1 79.4 us: home_shards(): rows = lax.all_gather(normed, both, axis=0, tiled=True)]
  transfers between devices with their start and end apart: 3 -> 5, of which waited for: 3 -> 4; matrix products, arithmetic and copies ran while one was open for 2% -> 5% of each run, Pallas kernels for 0% -> 5%
where the time goes in v1:
time: 824 us
  waiting for transfers between devices  487 us (59%)
  Pallas kernels  143 us (17%)
  blocking collectives  113 us (14%)
  local copies, waits for them, and re-layouts  37.9 us (5%)
  starting transfers between devices  15 us (2%)
  between operations  13.2 us (2%)
    reduce_scatter x1, waiting for transfers between devices, home_shards(): lax.psum_scatter(partial_value, both, scatter_dimension=0, tiled=True)  360 us
    pallas_call x1, Pallas kernels, routed_experts(): pl.pallas_call(lambda *refs: expert_kernel(*refs, capacity=capacity), out...  104 us
    all_gather x1, waiting for transfers between devices, home_shards(): rows = lax.all_gather(normed, both, axis=0, tiled=True)  79.4 us
    all_to_all x2, waiting for transfers between devices, exchanged(): return lax.all_to_all(blocks, axis, split_axis=0, concat_axis=0, tiled=True)  47.2 us
    all_gather x1, blocking collectives, home_shards(): all_routes = lax.all_gather(routes.T, both, axis=0, tiled=False)  41.2 us
    all_gather x1, blocking collectives, home_shards(): all_gates = lax.all_gather(route_gates.T, both, axis=0, tiled=False)  40.3 us
    pallas_call x1, Pallas kernels, paged_attention(): pl.pallas_call(lambda *refs: attention_kernel(*refs, heads=heads, step=st...  38.6 us
    unnamed x22, local copies, waits for them, and re-layouts  32.9 us
  transfers between devices with their start and end apart: 5, of which 4 were waited for; matrix products, arithmetic and copies ran while one was open for 5% of the time, Pallas kernels for 5%

profile of v1, /device:TPU:0, one launch (start us, length us, event | category | flops | bytes accessed | tf_op | source)
XLA Modules:
  0.0 824.0 jit_solution(14760033681742507619)
XLA Ops:
  6.5 0.7 all-gather.7.cloned.1.call-update
  7.3 1.0 select_reduce_fusion.1
  8.5 2.7 gather_fusion.2
  11.2 5.3 all-to-all-start
  16.7 0.6 gather_fusion.1
  17.9 34.7 %all-to-all-done.refs_3_ = bf16[4,1024,384]{2,1,0:T(8,128)(2,1)S(1)} async-done(((bf16[4,1024,384]{2,1,0:T(8,128)(2,1)}), bf16[4,1024,384]{2,1,0:T(8,128)(2,1)S(1)}, u32[]{:S(2)}, u32[]{:S(2)}) %all-to-all-start) | async-done | bytes 3145760 | tf_op jit(solution)/shard_map/all_to_all | solution.py:206
  52.6 38.6 %shard_map.127 = bf16[4,512,256]{2,1,0:T(8,128)(2,1)S(1)} custom-call(s32[4,64]{1,0:T(4,128)S(1)} %gather_fusion, s32[4]{0:T(128)S(1)} %gather_fusion.1, bf16[192,128,256]{2,1,0:T(8,128)(2,1)} %refs_2_.1, bf16[4,1024,384]{2,1,0:T(8,128)(2,1)S(1)} %all-to-all-done.refs_3_), custom_call_target="tpu_custom_call" | custom-call | tf_op jit(solution)/shard_map/pallas_call | solution.py:305
  91.2 1.0 copy-done.2
  92.2 9.7 %all-to-all-start.1 = ((bf16[4,512,256]{2,1,0:T(8,128)(2,1)}), bf16[4,512,256]{2,1,0:T(8,128)(2,1)S(1)}, u32[]{:S(2)}, u32[]{:S(2)}) async-start(bf16[4,512,256]{2,1,0:T(8,128)(2,1)} %copy-done.2), calls=%async_computation.1 | async-start | bytes 2097152 | tf_op jit(solution)/shard_map/all_to_all | solution.py:206
  102.0 12.6 %all-to-all-done.1 = bf16[4,512,256]{2,1,0:T(8,128)(2,1)S(1)} async-done(((bf16[4,512,256]{2,1,0:T(8,128)(2,1)}), bf16[4,512,256]{2,1,0:T(8,128)(2,1)S(1)}, u32[]{:S(2)}, u32[]{:S(2)}) %all-to-all-start.1) | async-done | bytes 1048608 | tf_op jit(solution)/shard_map/all_to_all | solution.py:206
  114.5 0.6 gather_fusion.3
  115.7 31.9 %all_to_all.29 = bf16[8,256,256]{1,2,0:T(8,128)(2,1)S(1)} all-to-all(bf16[8,256,256]{1,2,0:T(8,128)(2,1)S(1)} %copy.22), channel_id=1, replica_groups=mesh['dp'=4,'tensor'=8] {'tensor'}, dimensions={0} | all-to-all | bytes 2097152 | tf_op jit(solution)/shard_map/all_to_all | solution.py:452
  147.6 6.1 multiply_reduce_fusion
  153.7 1.4 multiply_convert_fusion
  155.3 16.2 %copy.23.refs_3_ = bf16[8,2048,352]{2,1,0:T(8,128)(2,1)} copy(bf16[8,2048,352]{1,2,0:T(8,128)(2,1)} %param.23) | data formatting | bytes 23068672 | tf_op args[10]
  171.5 15.5 %copy.24.refs_4_ = bf16[8,2048,352]{2,1,0:T(8,128)(2,1)} copy(bf16[8,2048,352]{1,2,0:T(8,128)(2,1)} %param.24) | data formatting | bytes 23068672 | tf_op args[11]
  187.0 41.2 %all-gather.2 = s32[32,6,256]{2,1,0:T(8,128)S(1)} all-gather(s32[1,6,256]{2,1,0:T(8,128)S(1)} %bitcast.43), channel_id=2, replica_groups=mesh['dp'=4,'tensor'=8] {'dp','tensor'}, dimensions={0}, use_global_device_ids=true | all-gather | bytes 202752 | tf_op jit(solution)/shard_map/all_gather | solution.py:461
  228.2 40.3 %all-gather.3 = f32[32,6,256]{2,1,0:T(8,128)S(1)} all-gather(f32[1,6,256]{2,1,0:T(8,128)S(1)} %bitcast.44), channel_id=3, replica_groups=mesh['dp'=4,'tensor'=8] {'dp','tensor'}, dimensions={0}, use_global_device_ids=true | all-gather | bytes 202752 | tf_op jit(solution)/shard_map/all_gather | solution.py:462
  268.9 1.0 fusion.refs_1_
  269.9 0.9 convolution_select_fusion.refs_0_
  270.8 79.4 %all-gather.9.cloned.1.call-done.refs_2_ = bf16[8192,2048]{1,0:T(8,128)(2,1)} async-done(((bf16[256,2048]{1,0:T(8,128)(2,1)}), bf16[8192,2048]{1,0:T(8,128)(2,1)}) %all-gather.9.cloned.1.call-update) | async-done | bytes 33554448 | tf_op jit(solution)/shard_map/all_gather | solution.py:474
  350.2 104.0 %shard_map.128 = bf16[8192,2048]{1,0:T(8,128)(2,1)} custom-call(f32[32,8,256]{2,1,0:T(8,128)} %convolution_select_fusion.refs_0_, f32[32,8,256]{2,1,0:T(8,128)} %fusion.refs_1_, bf16[8192,2048]{1,0:T(8,128)(2,1)} %all-gather.9.cloned.1.call-done.refs_2_, bf16[8,2048,352]{2,1,0:T(8,128)(2,1)} %copy.23.refs_3_, bf16[8,2048,352]{2,1,0:T(8,128)(2,1)} %copy.24.refs_4_, ...), custom_call_target="tpu_custom_call" | custom-call | tf_op jit(solution)/shard_map/pallas_call | solution.py:389
  454.3 359.7 %reduce-scatter.2.cloned.1.call-done = bf16[256,2048]{1,0:T(8,128)(2,1)} async-done(((bf16[8192,2048]{1,0:T(8,128)(2,1)}), bf16[256,2048]{1,0:T(8,128)(2,1)}) %reduce-scatter.2.cloned.1.call-update) | async-done | bytes 1048592 | tf_op jit(solution)/shard_map/reduce_scatter | solution.py:478
  814.0 3.5 convert_add_fusion
  (41 shorter events, 2.1 us)
Async XLA Ops:
  6.5 1.9 copy-start
  6.5 141.0 %all-gather.7.cloned.1.call-start = ((), (), s32[]{:S(2)}) async-start(), calls=%async_computation.4 | async-start | bytes 9437184 | tf_op jit(solution)/shard_map/all_gather | solution.py:451
  11.2 5.3 copy-start.9
  11.2 5.5 copy-start.3
  11.2 6.2 copy-start.5
  11.2 41.4 %all-to-all-start = ((bf16[4,1024,384]{2,1,0:T(8,128)(2,1)}), bf16[4,1024,384]{2,1,0:T(8,128)(2,1)S(1)}, u32[]{:S(2)}, u32[]{:S(2)}) async-start(bf16[4,1024,384]{2,1,0:T(8,128)(2,1)} %gather_fusion.2), calls=%async_computation | async-start | bytes 6291456 | tf_op jit(solution)/shard_map/all_to_all | solution.py:206
  91.2 1.0 copy-start.2
  92.2 22.3 %all-to-all-start.1 = ((bf16[4,512,256]{2,1,0:T(8,128)(2,1)}), bf16[4,512,256]{2,1,0:T(8,128)(2,1)S(1)}, u32[]{:S(2)}, u32[]{:S(2)}) async-start(bf16[4,512,256]{2,1,0:T(8,128)(2,1)} %copy-done.2), calls=%async_computation.1 | async-start | bytes 2097152 | tf_op jit(solution)/shard_map/all_to_all | solution.py:206
  101.9 248.3 %all-gather.9.cloned.1.call-start = ((), (), s32[]{:S(2)}) async-start(), calls=%async_computation.5 | async-start | bytes 34603008 | tf_op jit(solution)/shard_map/all_gather | solution.py:474
  147.6 6.1 copy-start.6
  153.6 1.7 copy-start.4
  155.3 658.7 %reduce-scatter.2.cloned.1.call-start = ((), (), s32[]{:S(2)}) async-start(), calls=%async_computation.6 | async-start | bytes 34603008 | tf_op jit(solution)/shard_map/reduce_scatter | solution.py:478
  171.5 15.5 %copy-start.7 = (s32[256,6]{0,1:T(8,128)S(1)}, s32[256,6]{0,1:T(8,128)}, u32[]{:S(2)}) copy-start(s32[256,6]{0,1:T(8,128)} %param.21) | copy-start | bytes 18436
  171.5 56.7 %copy-start.8 = (f32[256,6]{0,1:T(8,128)S(1)}, f32[256,6]{0,1:T(8,128)}, u32[]{:S(2)}) copy-start(f32[256,6]{0,1:T(8,128)} %param.22) | copy-start | bytes 18436
  454.2 363.3 %copy-start.1 = (bf16[4,1024,384]{2,1,0:T(8,128)(2,1)S(1)}, bf16[4,1024,384]{2,1,0:T(8,128)(2,1)}, u32[]{:S(2)}) copy-start(bf16[4,1024,384]{2,1,0:T(8,128)(2,1)} %param.17) | copy-start | bytes 9437188
Sparse Core Ops, SparseCore 0:
  9.0 84.7 all-gather.6
  155.2 194.9 all-gather.8
  454.4 359.5 reduce-scatter.1
